TPU v7x, 32 devices: a whole 2x2x4 slice. The times are simulated.
32 devices in a mesh: depth: 4 (over x, core), height: 2 (over y), sample: 4 (over z).
Axes of the slice: x: 2, y: 2, z: 4, core: 2. Of those that a mesh axis runs over, the one named last changes fastest.
Arguments:
- volume: bfloat16 [4, 4, 16, 8, 512], P('sample', None, 'depth', 'height'), may hold values from -6 to 6
- kernel_one: bfloat16 [32, 108], replicated, may hold values from -0.625 to 0.625
- kernel_two: bfloat16 [64, 864], P('height'), may hold values from -0.21875 to 0.21875
- cotangent: bfloat16 [4, 64, 4, 256], P('sample', 'height', 'depth'), may hold values from -24 to 24
Outputs:
- pooled_two: bfloat16 [4, 64, 4, 256], P('sample', 'height', 'depth')
- weight_grad: float32 [64, 864], P('height')
- act_grad: bfloat16 [4, 32, 8, 4, 256], P('sample', None, 'depth', 'height')
All inputs are finite; a program needn't handle non-finite values.
Results may differ from a plain program's by a relative error of at most 0.005.
Values may be sent and summed in bfloat16 or wider, within the bound.
A program may use at most 64 MiB of HBM per device.

v0:
```python
import functools

import jax
import jax.numpy as jnp
import numpy as np
from jax import lax
from jax.experimental import pallas as pl
from jax.experimental.pallas import tpu as pltpu
from jax.sharding import PartitionSpec as P

LEAK_SLOPE = 0.3
CONV_DIMS = ("NCDHW", "OIDHW", "NCDHW")


def extended(block, sides, width):
    for axis, dim in sides:
        count = lax.axis_size(axis)
        forward = [(i, i + 1) for i in range(count - 1)]
        backward = [(target, source) for source, target in forward]
        low = lax.ppermute(
            lax.slice_in_dim(block, block.shape[dim] - width, None, axis=dim), axis, forward
        )
        high = lax.ppermute(lax.slice_in_dim(block, 0, width, axis=dim), axis, backward)
        block = jnp.concatenate([low, block, high], axis=dim)
    return block


def activate(values):
    return LEAK_SLOPE * values + (1.0 - LEAK_SLOPE) * jax.nn.softplus(values)


def slope_at(values):
    return LEAK_SLOPE + (1.0 - LEAK_SLOPE) * jax.nn.sigmoid(values)


def pooled(values):
    count, chans, dsize, hsize, wsize = values.shape
    blocks = values.reshape(count, chans, dsize // 2, 2, hsize // 2, 2, wsize // 2, 2)
    return blocks.mean(axis=(3, 5, 7))


def spread_up(values):
    values = jnp.repeat(jnp.repeat(jnp.repeat(values, 2, axis=2), 2, axis=3), 2, axis=4)
    return values * 0.125


def conv_valid(inputs, kernel):
    return lax.conv_general_dilated(
        inputs,
        kernel,
        (1, 1, 1),
        "VALID",
        dimension_numbers=CONV_DIMS,
        preferred_element_type=jnp.float32,
    )


def back_conv(delta_pad, kernel):
    flipped = jnp.flip(kernel, axis=(2, 3, 4))
    return lax.conv_general_dilated(
        delta_pad,
        flipped,
        (1, 1, 1),
        "VALID",
        dimension_numbers=("NCDHW", "IODHW", "NCDHW"),
        preferred_element_type=jnp.float32,
    )


def shards(volume, kernel_one, kernel_two, cotangent):
    depth_count = lax.axis_size("depth")
    height_count = lax.axis_size("height")
    sample_count = lax.axis_size("sample")
    chans_in = volume.shape[1]
    depth_loc = volume.shape[2]
    height_loc = volume.shape[3]
    width_all = volume.shape[4]
    chans_mid = kernel_one.shape[0]
    filters = kernel_two.shape[0]
    first_kernel = kernel_one.reshape(chans_mid, chans_in, 3, 3, 3)
    second_kernel = kernel_two.reshape(filters, chans_mid, 3, 3, 3)
    padded = extended(volume, (("depth", 2), ("height", 3)), 1)
    window = jnp.pad(padded, ((0, 0), (0, 0), (0, 0), (0, 0), (1, 1)))
    level_loc = pooled(activate(conv_valid(window, first_kernel))).astype(jnp.bfloat16)
    slab_rows = lax.all_gather(level_loc, "height", axis=3, tiled=True)
    level_one = extended(slab_rows, (("depth", 2),), 1)
    level_pad = jnp.pad(level_one, ((0, 0), (0, 0), (0, 0), (1, 1), (1, 1)))
    pre_two = conv_valid(level_pad, second_kernel)
    pooled_grid = pooled(activate(pre_two)).astype(jnp.bfloat16)
    depth_two = pooled_grid.shape[2]
    pooled_two = pooled_grid.reshape(
        1, filters, depth_two, pooled_grid.shape[3] * pooled_grid.shape[4]
    )
    cot_grid = cotangent.reshape(1, filters, depth_two, pooled_grid.shape[3], pooled_grid.shape[4])
    delta_two = (spread_up(cot_grid.astype(jnp.float32)) * slope_at(pre_two)).astype(jnp.bfloat16)
    weight_part = lax.conv_general_dilated(
        level_pad,
        delta_two,
        (1, 1, 1),
        "VALID",
        dimension_numbers=("CNDHW", "IODHW", "NCDHW"),
        preferred_element_type=jnp.float32,
    )
    total_cells = (
        sample_count
        * (depth_loc // 2)
        * depth_count
        * (height_loc // 2)
        * height_count
        * (width_all // 2)
    )
    scale = 1.0 / float(total_cells) ** 0.5
    weight_term = jnp.transpose(weight_part * scale, (1, 0, 2, 3, 4)).reshape(
        filters, chans_mid * 27
    )
    weight_grad = lax.psum(weight_term, ("depth", "sample"))
    delta_ext = extended(delta_two, (("depth", 2),), 1)
    delta_pad = jnp.pad(delta_ext, ((0, 0), (0, 0), (0, 0), (1, 1), (1, 1)))
    back_part = back_conv(delta_pad, second_kernel)
    act_grad = lax.psum_scatter(back_part, "height", scatter_dimension=3, tiled=True).astype(
        jnp.bfloat16
    )
    return (pooled_two, weight_grad, act_grad)


BF16 = jnp.bfloat16
F32 = jnp.float32
MESH = pl.DeviceIdType.MESH


def constants():
    parts = np.zeros((512, 6, 128), np.float32)
    for step in range(6):
        for cell in range(128):
            w = 4 * cell - 1 + step
            if 0 <= w < 512:
                parts[w, step, cell] = 1
    order = np.zeros((4, 8, 4, 6, 4, 4), np.float32)
    for step in range(6):
        for h in range(4):
            for c in range(4):
                order[h, step, c, step, h, c] = 1
    first = np.zeros((4, 3, 3, 3, 4, 4, 8, 4), np.float32)
    second = np.zeros((32, 3, 3, 3, 3, 3, 4, 32), np.float32)
    for i in range(3):
        for j in range(3):
            for k in range(3):
                for c in range(4):
                    first[c, i, j, k, i, j, k, c] = 1
                for c in range(32):
                    second[c, i, j, k, i, j, k, c] = 1
    second = np.pad(second.reshape(864, 1152), ((0, 160), (0, 0)))
    weave = np.zeros((2, 128, 256), np.float32)
    for q in range(2):
        for cell in range(128):
            weave[q, cell, 2 * cell + q] = 1
    rows = np.zeros((32, 4, 4, 32), np.float32)
    for c in range(32):
        for place in range(4):
            rows[c, place, place, c] = 1
    shaped = (
        parts.reshape(512, 768),
        order.reshape(128, 96),
        first.reshape(108, 512),
        second,
        weave.reshape(256, 256),
        rows.reshape(128, 128),
    )
    return [jnp.asarray(item, BF16) for item in shaped]


def dot(a, b):
    return jnp.dot(a, b, preferred_element_type=F32)


def dot_nt(a, b):
    return lax.dot_general(a, b, (((1,), (1,)), ((), ())), preferred_element_type=F32)


def lane_shift(values, by):
    lanes = values.shape[1]
    lane = lax.broadcasted_iota(jnp.int32, values.shape, 1)
    if by > 0:
        return jnp.where(lane >= by, pltpu.roll(values, by, 1), 0.0)
    return jnp.where(lane < lanes + by, pltpu.roll(values, lanes + by, 1), 0.0)


def kernel(
    counts, scale,
    vol, k1, k2, cot, parts, order, first, second, weave, rows,
    pooled_out, weight_out, act_out,
    raw, k2_far, cots, grid, level, delta, amat, bmat, bmat_t, wpart, wrecv, wgath,
    vol_send, vol_recv, cot_send, cot_recv, k2_send, k2_recv, w_send, w_recv, g_send, g_recv,
):
    depth_count, sample_count = counts
    group = depth_count * sample_count
    D = lax.axis_index("depth")
    H = lax.axis_index("height")
    S = lax.axis_index("sample")
    me = D * sample_count + S

    def device(d, h, s):
        return {"depth": d, "height": h, "sample": s}

    barrier = pltpu.get_barrier_semaphore()
    for step in range(1, depth_count):
        other = lax.rem(D + step, depth_count)
        for far in range(2):
            h = H if far == 0 else 1 - H
            pl.semaphore_signal(barrier, inc=1, device_id=device(other, h, S), device_id_type=MESH)
    pl.semaphore_signal(barrier, inc=1, device_id=device(D, 1 - H, S), device_id_type=MESH)
    for d_step in range(depth_count):
        for s_step in range(1, sample_count):
            pl.semaphore_signal(
                barrier, inc=1, device_id_type=MESH,
                device_id=device(
                    lax.rem(D + d_step, depth_count), H, lax.rem(S + s_step, sample_count)
                ),
            )
    pl.semaphore_wait(barrier, 2 * depth_count - 1 + depth_count * (sample_count - 1))

    def vol_copy(step, far, owner_h):
        if step == 2:
            src, dst = vol.at[3:4], raw.at[owner_h, 0:1]
        elif step == -2:
            src, dst = vol.at[0:1], raw.at[owner_h, 13:14]
        else:
            start = 5 - 4 * step
            src, dst = vol, raw.at[owner_h, start:start + 4]
        slot = (step + 2) * 2 + far
        return pltpu.make_async_remote_copy(
            src_ref=src, dst_ref=dst, send_sem=vol_send.at[slot], recv_sem=vol_recv.at[slot],
            device_id=device(D + step, H if far == 0 else 1 - H, S), device_id_type=MESH,
        )

    def cot_copy(step, far):
        slot = (step + 1) * 2 + far
        return pltpu.make_async_remote_copy(
            src_ref=cot, dst_ref=cots.at[far, 1 - step],
            send_sem=cot_send.at[slot], recv_sem=cot_recv.at[slot],
            device_id=device(D + step, H if far == 0 else 1 - H, S), device_id_type=MESH,
        )

    k2_copy = pltpu.make_async_remote_copy(
        src_ref=k2, dst_ref=k2_far, send_sem=k2_send.at[0], recv_sem=k2_recv.at[0],
        device_id=device(D, 1 - H, S), device_id_type=MESH,
    )
    vol_kinds = [(s, f) for s in (0, 1, -1, 2, -2) for f in (1, 0) if (s, f) != (0, 0)]
    cot_kinds = [(s, f) for s in (0, 1, -1) for f in (1, 0) if (s, f) != (0, 0)]

    def goes(step):
        return jnp.logical_and(D + step >= 0, D + step < depth_count)

    def comes(step):
        return jnp.logical_and(D - step >= 0, D - step < depth_count)

    for step, far in vol_kinds:
        @pl.when(goes(step))
        def _():
            vol_copy(step, far, H).start()
    k2_copy.start()
    for step, far in cot_kinds:
        @pl.when(goes(step))
        def _():
            cot_copy(step, far).start()

    raw[H, 5:9] = vol[...]
    cots[0, 1] = cot[...]
    for step in (1, 2, -1, -2):
        low, high = {1: (1, 5), 2: (0, 1), -1: (9, 13), -2: (13, 14)}[step]

        @pl.when(jnp.logical_not(comes(step)))
        def _():
            raw[:, low:high] = jnp.zeros((2, high - low, 16, 512), BF16)
            if abs(step) == 1:
                cots[0, 1 - step] = jnp.zeros((32, 256), BF16)
                cots[1, 1 - step] = jnp.zeros((32, 256), BF16)
    grid[:, 0] = jnp.zeros((14, 32, 128), BF16)
    grid[:, 9] = jnp.zeros((14, 32, 128), BF16)
    level[:, 0] = jnp.zeros((6, 128, 128), BF16)
    level[:, 5] = jnp.zeros((6, 128, 128), BF16)
    delta[:, 0] = jnp.zeros((4, 128, 128), BF16)
    delta[:, 5] = jnp.zeros((4, 128, 128), BF16)

    base = dot(k1[...], first[...])
    for wp in range(4):
        for dp in range(2):
            for hp in range(2):
                by = dp * 128 + hp * 32 + wp * 4
                row = (wp // 2) * 256 + ((wp % 2) * 4 + dp * 2 + hp) * 32
                turned = base if by == 0 else pltpu.roll(base, by, 1)
                amat[row:row + 32, :] = turned.astype(BF16)

    def spread_kernel(values, far):
        wide = dot(values, second[0:864, :])
        bmat[far * 32:far * 32 + 32, :] = wide.astype(BF16)
        bmat[64 + far * 32:96 + far * 32, :] = pltpu.roll(wide, 32, 1).astype(BF16)

    spread_kernel(k2[...], 0)

    for step, far in vol_kinds:
        @pl.when(comes(step))
        def _():
            vol_copy(step, far, H if far == 0 else 1 - H).wait_recv()

    def split_row(r, carry):
        both = jnp.concatenate([raw[0, r], raw[1, r]], axis=0)
        cut = dot(both, parts[...]).astype(BF16)
        stacked = jnp.concatenate(
            [
                jnp.concatenate(
                    [cut[h * 16:h * 16 + 16, s * 128:s * 128 + 128] for h in range(2)], axis=1
                )
                for s in range(6)
            ],
            axis=0,
        )
        placed = dot(order[...], stacked).astype(BF16)
        for h in range(8):
            grid[r, 1 + h] = placed[(h % 4) * 32:(h % 4) * 32 + 32, (h // 4) * 128:(h // 4) * 128 + 128]
        return carry

    lax.fori_loop(0, 14, split_row, 0)

    def first_layer(ld, carry):
        here = 2 * D - 2 + ld
        inside = jnp.logical_and(here >= 0, here < 2 * depth_count)
        for pair in range(2):
            cells = jnp.concatenate(
                [
                    grid[pl.ds(2 * ld, 4), 2 * lh:2 * lh + 4].reshape(512, 128)
                    for lh in (2 * pair, 2 * pair + 1)
                ],
                axis=1,
            )
            halves = []
            for q in range(2):
                z = dot(amat[q * 256:q * 256 + 256, :], cells)
                line = jnp.maximum(z, LEAK_SLOPE * z)
                more = 1.0 + jnp.exp(-jnp.abs(z))
                total = line[0:32]
                product = more[0:32]
                for i in range(1, 8):
                    total = total + line[32 * i:32 * i + 32]
                    product = product * more[32 * i:32 * i + 32]
                value = 0.125 * (total + (1.0 - LEAK_SLOPE) * jnp.log(product))
                halves.append(jnp.where(inside, value, 0.0))
            for i in range(2):
                even = halves[0][:, i * 128:i * 128 + 128]
                odd = halves[1][:, i * 128:i * 128 + 128]
                level[ld, 1 + 2 * pair + i] = jnp.concatenate(
                    [lane_shift(odd, 1), even, odd, lane_shift(even, -1)], axis=0
                ).astype(BF16)
        return carry

    lax.fori_loop(0, 6, first_layer, 0)

    k2_copy.wait_recv()
    spread_kernel(k2_far[...], 1)
    for step, far in cot_kinds:
        @pl.when(comes(step))
        def _():
            cot_copy(step, far).wait_recv()
    for kk in range(9):
        tile = bmat[:, kk * 128:kk * 128 + 128].astype(F32)
        bmat_t[:, kk * 128:kk * 128 + 128] = tile.T.astype(BF16)

    for pair in range(2):
        pool_line = jnp.zeros((32, 128), F32)
        pool_more = jnp.ones((32, 128), F32)
        for dd in range(4):
            cells = jnp.concatenate(
                [level[dd:dd + 3, lh:lh + 3].reshape(1152, 128) for lh in (2 * pair, 2 * pair + 1)],
                axis=1,
            )
            z = dot(bmat[...], cells)
            small = jnp.exp(-jnp.abs(z))
            more = 1.0 + small
            turn = 1.0 / more
            slope = LEAK_SLOPE + (1.0 - LEAK_SLOPE) * jnp.where(z >= 0, turn, small * turn)
            if dd in (1, 2):
                line = jnp.maximum(z, LEAK_SLOPE * z)
                for wp in range(2):
                    for i in range(2):
                        box = (slice(wp * 64, wp * 64 + 32), slice(i * 128, i * 128 + 128))
                        pool_line = pool_line + line[box]
                        pool_more = pool_more * more[box]
            at = (dd + 1) // 2
            near = cots[0, at, :, pair * 128:pair * 128 + 128].astype(F32)
            away = cots[1, at, :, pair * 128:pair * 128 + 128].astype(F32)
            grad = jnp.concatenate([near, away, near, away], axis=0) * 0.125
            for i in range(2):
                delta[dd, 1 + 2 * pair + i] = (grad * slope[:, i * 128:i * 128 + 128]).astype(BF16)
        value = 0.125 * (pool_line + (1.0 - LEAK_SLOPE) * jnp.log(pool_more))
        pooled_out[:, pair * 128:pair * 128 + 128] = value.astype(BF16)

    spots = [(dd, lh) for dd in (1, 2) for lh in range(4)]
    mine = jnp.concatenate(
        [
            jnp.concatenate([delta[dd, 1 + lh, 0:32], delta[dd, 1 + lh, 64:96]], axis=0)
            for dd, lh in spots
        ],
        axis=1,
    )
    folded = []
    for kd in range(3):
        for kh in range(3):
            cells = jnp.concatenate([level[dd + kd, lh + kh] for dd, lh in spots], axis=1)
            terms = dot_nt(mine, cells)
            folded.append(terms[0:32] + pltpu.roll(terms[32:64], 96, 1))
    sums = jnp.concatenate(folded, axis=1)
    coarse = sums.astype(BF16)
    fine = (sums - coarse.astype(F32)).astype(BF16)
    ordered = dot_nt(jnp.concatenate([coarse, fine], axis=0), second[...])
    ordered = (ordered[0:32] + ordered[32:64]) * scale
    for r in range(4):
        for q in range(4):
            wpart[r * 4 + q] = ordered[r * 8:r * 8 + 8, q * 256:q * 256 + 256]

    def peer(i):
        other = lax.rem(me + i, group)
        return other, device(other // sample_count, H, lax.rem(other, sample_count))

    def w_copy(i):
        other, where = peer(i)
        return pltpu.make_async_remote_copy(
            src_ref=wpart.at[other], dst_ref=wrecv.at[i], send_sem=w_send.at[i],
            recv_sem=w_recv.at[i], device_id=where, device_id_type=MESH,
        )

    def g_copy(i):
        other, where = peer(i)
        return pltpu.make_async_remote_copy(
            src_ref=wgath.at[me], dst_ref=wgath.at[me], send_sem=g_send.at[i],
            recv_sem=g_recv.at[i], device_id=where, device_id_type=MESH,
        )

    def g_arrival(i):
        other = lax.rem(me + group - i, group)
        return pltpu.make_async_remote_copy(
            src_ref=wgath.at[other], dst_ref=wgath.at[other], send_sem=g_send.at[i],
            recv_sem=g_recv.at[i], device_id=device(D, 1 - H, S), device_id_type=MESH,
        )

    def each(call):
        def body(i, carry):
            call(i)
            return carry

        lax.fori_loop(1, group, body, 0)

    each(lambda i: w_copy(i).start())

    found = []
    for od in range(2):
        cells = jnp.concatenate(
            [
                jnp.concatenate(
                    [
                        delta[od + 2 - kd, 2 * H + oh + 2 - kh]
                        for kd in range(3)
                        for kh in range(3)
                    ],
                    axis=0,
                )
                for oh in range(2)
            ],
            axis=1,
        )
        back = dot(bmat_t[...], cells)
        for oh in range(2):
            one = back[:, oh * 128:oh * 128 + 128]
            even = one[32:64] + lane_shift(one[96:128], 1)
            odd = one[64:96] + lane_shift(one[0:32], -1)
            found.append(jnp.concatenate([even, odd], axis=1).astype(BF16))
    woven = dot(jnp.concatenate(found, axis=0), weave[...]).astype(BF16)
    act_out[...] = dot(rows[...], woven).astype(BF16)

    each(lambda i: w_copy(i).wait_recv())
    chunk = wpart[me]
    for i in range(1, group):
        chunk = chunk + wrecv[i]
    wgath[me] = chunk
    each(lambda i: g_copy(i).start())
    each(lambda i: g_arrival(i).wait_recv())
    for r in range(4):
        for q in range(3):
            weight_out[r * 8:r * 8 + 8, q * 256:q * 256 + 256] = wgath[r * 4 + q]
        weight_out[r * 8:r * 8 + 8, 768:864] = wgath[r * 4 + 3, :, 0:96]

    each(lambda i: w_copy(i).wait_send())
    each(lambda i: g_copy(i).wait_send())
    for step, far in vol_kinds:
        @pl.when(goes(step))
        def _():
            vol_copy(step, far, H).wait_send()
    k2_copy.wait_send()
    for step, far in cot_kinds:
        @pl.when(goes(step))
        def _():
            cot_copy(step, far).wait_send()


def one_kernel(volume, kernel_one, kernel_two, cotangent):
    depth_count = lax.axis_size("depth")
    sample_count = lax.axis_size("sample")
    group = depth_count * sample_count
    total_cells = sample_count * 2 * depth_count * 4 * 256
    scale = 1.0 / float(total_cells) ** 0.5
    vol = jnp.transpose(volume[0], (1, 2, 0, 3)).reshape(4, 16, 512)
    vmem = pl.BlockSpec(memory_space=pltpu.VMEM)
    dma = pltpu.SemaphoreType.DMA
    pooled_two, weight_grad, act = pl.pallas_call(
        functools.partial(kernel, (depth_count, sample_count), scale),
        out_shape=(
            jax.ShapeDtypeStruct((32, 256), BF16),
            jax.ShapeDtypeStruct((32, 864), F32),
            jax.ShapeDtypeStruct((128, 256), BF16),
        ),
        in_specs=[vmem] * 10,
        out_specs=(vmem,) * 3,
        scratch_shapes=[
            pltpu.VMEM((2, 14, 16, 512), BF16),
            pltpu.VMEM((32, 864), BF16),
            pltpu.VMEM((2, 3, 32, 256), BF16),
            pltpu.VMEM((14, 10, 32, 128), BF16),
            pltpu.VMEM((6, 6, 128, 128), BF16),
            pltpu.VMEM((4, 6, 128, 128), BF16),
            pltpu.VMEM((512, 512), BF16),
            pltpu.VMEM((128, 1152), BF16),
            pltpu.VMEM((128, 1152), BF16),
            pltpu.VMEM((group, 8, 256), F32),
            pltpu.VMEM((group, 8, 256), F32),
            pltpu.VMEM((group, 8, 256), F32),
            dma((10,)), dma((10,)), dma((6,)), dma((6,)), dma((1,)), dma((1,)),
            dma((group,)), dma((group,)), dma((group,)), dma((group,)),
        ],
        compiler_params=pltpu.CompilerParams(
            collective_id=0, has_side_effects=True, vmem_limit_bytes=40 * 1024 * 1024
        ),
    )(vol, kernel_one, kernel_two, cotangent.reshape(32, 256), *constants())
    return (
        pooled_two.reshape(1, 32, 1, 256),
        weight_grad,
        act.reshape(1, 32, 2, 2, 256),
    )


def solution(mesh):
    in_specs = (
        P("sample", None, "depth", "height", None),
        P(),
        P("height", None),
        P("sample", "height", "depth", None),
    )
    out_specs = (
        P("sample", "height", "depth", None),
        P("height", None),
        P("sample", None, "depth", "height", None),
    )
    fits = mesh.shape["height"] == 2 and mesh.shape["depth"] * mesh.shape["sample"] == 16
    body = one_kernel if fits else shards
    return jax.shard_map(body, mesh=mesh, in_specs=in_specs, out_specs=out_specs, check_vma=False)
```

profile of v0, /device:TPU:0, one launch (start us, length us, event | category | flops | bytes accessed | tf_op | source)
XLA Modules:
  0.0 48.0 jit_solution(10256344702189524158)
XLA Ops:
  0.6 0.9 %copy.13 = bf16[4,4,4,512]{3,2,1,0:T(4,128)(2,1)S(1)} copy(bf16[4,4,4,512]{3,1,0,2:T(4,128)(2,1)} %bitcast.7) | data formatting | bytes 131072 | tf_op jit(solution)/shard_map/transpose | solution.py:510
  1.5 0.0 copy-start
  1.6 1.7 %copy-done = bf16[1024,1152]{1,0:T(8,128)(2,1)S(1)} copy-done((bf16[1024,1152]{1,0:T(8,128)(2,1)S(1)}, bf16[1024,1152]{1,0:T(8,128)(2,1)}, u32[]{:S(2)}) %copy-start) | copy-done | bytes 2359320
  3.2 0.0 copy-start.1
  3.2 1.1 %copy-done.1 = bf16[512,768]{1,0:T(8,128)(2,1)S(1)} copy-done((bf16[512,768]{1,0:T(8,128)(2,1)S(1)}, bf16[512,768]{1,0:T(8,128)(2,1)}, u32[]{:S(2)}) %copy-start.1) | copy-done | bytes 786456
  4.4 0.0 copy-start.2
  4.4 0.9 %copy-done.2 = bf16[256,256]{1,0:T(8,128)(2,1)S(1)} copy-done((bf16[256,256]{1,0:T(8,128)(2,1)S(1)}, bf16[256,256]{1,0:T(8,128)(2,1)}, u32[]{:S(2)}) %copy-start.2) | copy-done | bytes 131096
  5.3 0.0 copy-start.3
  5.3 0.9 %copy-done.3 = bf16[108,512]{1,0:T(8,128)(2,1)S(1)} copy-done((bf16[108,512]{1,0:T(8,128)(2,1)S(1)}, bf16[108,512]{1,0:T(8,128)(2,1)}, u32[]{:S(2)}) %copy-start.3) | copy-done | bytes 110616
  6.2 0.0 copy-start.4
  6.2 0.8 %copy-done.4 = bf16[32,864]{1,0:T(8,128)(2,1)S(1)} copy-done((bf16[32,864]{1,0:T(8,128)(2,1)S(1)}, bf16[32,864]{1,0:T(8,128)(2,1)}, u32[]{:S(2)}) %copy-start.4) | copy-done | bytes 55320
  7.0 0.0 copy-start.5
  7.0 0.8 %copy-done.5 = bf16[128,128]{1,0:T(8,128)(2,1)S(1)} copy-done((bf16[128,128]{1,0:T(8,128)(2,1)S(1)}, bf16[128,128]{1,0:T(8,128)(2,1)}, u32[]{:S(2)}) %copy-start.5) | copy-done | bytes 32792
  7.7 0.0 copy-start.6
  7.7 0.8 %copy-done.6 = bf16[128,96]{1,0:T(8,128)(2,1)S(1)} copy-done((bf16[128,96]{1,0:T(8,128)(2,1)S(1)}, bf16[128,96]{1,0:T(8,128)(2,1)}, u32[]{:S(2)}) %copy-start.6) | copy-done | bytes 24600
  8.5 0.0 copy-start.7
  8.5 0.7 %copy-done.7 = bf16[1,32,1,256]{3,1,2,0:T(8,128)(2,1)S(1)} copy-done((bf16[1,32,1,256]{3,1,2,0:T(8,128)(2,1)S(1)}, bf16[1,32,1,256]{3,1,2,0:T(8,128)(2,1)}, u32[]{:S(2)}) %copy-start.7) | copy-done | bytes 16408
  9.2 0.0 copy-start.8
  9.2 0.7 %copy-done.8 = bf16[32,108]{1,0:T(8,128)(2,1)S(1)} copy-done((bf16[32,108]{1,0:T(8,128)(2,1)S(1)}, bf16[32,108]{1,0:T(8,128)(2,1)}, u32[]{:S(2)}) %copy-start.8) | copy-done | bytes 6936
  9.9 36.2 %shard_map.121 = (bf16[32,256]{1,0:T(8,128)(2,1)S(1)}, f32[32,864]{1,0:T(8,128)S(1)}, bf16[128,256]{1,0:T(8,128)(2,1)S(1)}) custom-call(bf16[4,16,512]{2,1,0:T(8,128)(2,1)S(1)} %reshape.18.vol, bf16[32,108]{1,0:T(8,128)(2,1)S(1)} %copy-done.8, bf16[32,864]{1,0:T(8,128)(2,1)S(1)} %copy-done.4, bf16[32,256]{1,0:T(8,128)(2,1)S(1)} %bitcast.5, ...), custom_call_target="tpu_custom_call" | custom-call | tf_op jit(solution)/shard_map/pallas_call | solution.py:513
  46.1 0.7 %reshape.21 = bf16[1,32,2,2,256]{4,3,2,1,0:T(2,128)(2,1)} reshape(bf16[128,256]{1,0:T(8,128)(2,1)S(1)} %get-tuple-element.8) | data formatting | bytes 131072 | tf_op jit(solution)/shard_map/reshape | solution.py:545
  46.8 0.6 %copy.16 = bf16[1,32,1,256]{3,1,2,0:T(8,128)(2,1)} copy(bf16[1,32,1,256]{3,1,2,0:T(8,128)(2,1)S(1)} %bitcast.6) | data formatting | bytes 32768
  47.4 0.6 %copy.17 = f32[32,864]{1,0:T(8,128)} copy(f32[32,864]{1,0:T(8,128)S(1)} %get-tuple-element.13) | data formatting | bytes 221184
  (1 shorter events, 0.0 us)
Async XLA Ops:
  1.5 1.7 %copy-start = (bf16[1024,1152]{1,0:T(8,128)(2,1)S(1)}, bf16[1024,1152]{1,0:T(8,128)(2,1)}, u32[]{:S(2)}) copy-start(bf16[1024,1152]{1,0:T(8,128)(2,1)} %constant.15.clone.second) | copy-start | bytes 7077892
  3.2 1.1 %copy-start.1 = (bf16[512,768]{1,0:T(8,128)(2,1)S(1)}, bf16[512,768]{1,0:T(8,128)(2,1)}, u32[]{:S(2)}) copy-start(bf16[512,768]{1,0:T(8,128)(2,1)} %constant.12.clone.parts) | copy-start | bytes 2359300
  4.4 0.9 %copy-start.2 = (bf16[256,256]{1,0:T(8,128)(2,1)S(1)}, bf16[256,256]{1,0:T(8,128)(2,1)}, u32[]{:S(2)}) copy-start(bf16[256,256]{1,0:T(8,128)(2,1)} %constant.16.clone.weave) | copy-start | bytes 393220
  5.3 0.9 %copy-start.3 = (bf16[108,512]{1,0:T(8,128)(2,1)S(1)}, bf16[108,512]{1,0:T(8,128)(2,1)}, u32[]{:S(2)}) copy-start(bf16[108,512]{1,0:T(8,128)(2,1)} %constant.14.clone.first) | copy-start | bytes 331780
  6.2 0.8 %copy-start.4 = (bf16[32,864]{1,0:T(8,128)(2,1)S(1)}, bf16[32,864]{1,0:T(8,128)(2,1)}, u32[]{:S(2)}) copy-start(bf16[32,864]{1,0:T(8,128)(2,1)} %k2.1) | copy-start | bytes 165892
  7.0 0.8 %copy-start.5 = (bf16[128,128]{1,0:T(8,128)(2,1)S(1)}, bf16[128,128]{1,0:T(8,128)(2,1)}, u32[]{:S(2)}) copy-start(bf16[128,128]{1,0:T(8,128)(2,1)} %constant.17.clone.rows) | copy-start | bytes 98308
  7.7 0.8 %copy-start.6 = (bf16[128,96]{1,0:T(8,128)(2,1)S(1)}, bf16[128,96]{1,0:T(8,128)(2,1)}, u32[]{:S(2)}) copy-start(bf16[128,96]{1,0:T(8,128)(2,1)} %constant.13.clone.order) | copy-start | bytes 73732
  8.5 0.7 %copy-start.7 = (bf16[1,32,1,256]{3,1,2,0:T(8,128)(2,1)S(1)}, bf16[1,32,1,256]{3,1,2,0:T(8,128)(2,1)}, u32[]{:S(2)}) copy-start(bf16[1,32,1,256]{3,1,2,0:T(8,128)(2,1)} %param.13) | copy-start | bytes 49156
  9.2 0.7 %copy-start.8 = (bf16[32,108]{1,0:T(8,128)(2,1)S(1)}, bf16[32,108]{1,0:T(8,128)(2,1)}, u32[]{:S(2)}) copy-start(bf16[32,108]{1,0:T(8,128)(2,1)} %k1.1) | copy-start | bytes 20740
where the time goes:
time: 48.6 us; the launch traced here: 48 us
  Pallas kernels  36.2 us (74%)
  local copies, waits for them, and re-layouts  11.2 us (23%)
  between operations  0.66 us (1%)
    pallas_call x1, Pallas kernels, one_kernel(): pl.pallas_call(functools.partial(kernel, (depth_count, sample_count), sca...  36.2 us
    unnamed x20, local copies, waits for them, and re-layouts  9.59 us

commit v1 on v0

--- a/solution.py
+++ b/solution.py
@@ -187,9 +187,10 @@
 
 def kernel(
     counts, scale,
-    vol, k1, k2, cot, parts, order, first, second, weave, rows,
+    vol, k1_hbm, k2_hbm, cot_hbm, parts_hbm, order_hbm, first_hbm, second_hbm, weave_hbm, rows_hbm,
     pooled_out, weight_out, act_out,
     raw, k2_far, cots, grid, level, delta, amat, bmat, bmat_t, wpart, wrecv, wgath,
+    k1, k2, parts, order, first, second, weave, rows, local,
     vol_send, vol_recv, cot_send, cot_recv, k2_send, k2_recv, w_send, w_recv, g_send, g_recv,
 ):
     depth_count, sample_count = counts
@@ -217,6 +218,20 @@
                     lax.rem(D + d_step, depth_count), H, lax.rem(S + s_step, sample_count)
                 ),
             )
+    loads = {
+        name: pltpu.make_async_copy(src, dst, local.at[i])
+        for i, (name, src, dst) in enumerate(
+            [
+                ("k1", k1_hbm, k1), ("first", first_hbm, first), ("k2", k2_hbm, k2),
+                ("second", second_hbm, second), ("parts", parts_hbm, parts),
+                ("order", order_hbm, order), ("cot", cot_hbm, cots.at[0, 1]),
+                ("weave", weave_hbm, weave), ("rows", rows_hbm, rows),
+            ]
+        )
+    }
+    for load in loads.values():
+        load.start()
+
     pl.semaphore_wait(barrier, 2 * depth_count - 1 + depth_count * (sample_count - 1))
 
     def vol_copy(step, far, owner_h):
@@ -236,13 +251,13 @@
     def cot_copy(step, far):
         slot = (step + 1) * 2 + far
         return pltpu.make_async_remote_copy(
-            src_ref=cot, dst_ref=cots.at[far, 1 - step],
+            src_ref=cot_hbm, dst_ref=cots.at[far, 1 - step],
             send_sem=cot_send.at[slot], recv_sem=cot_recv.at[slot],
             device_id=device(D + step, H if far == 0 else 1 - H, S), device_id_type=MESH,
         )
 
     k2_copy = pltpu.make_async_remote_copy(
-        src_ref=k2, dst_ref=k2_far, send_sem=k2_send.at[0], recv_sem=k2_recv.at[0],
+        src_ref=k2_hbm, dst_ref=k2_far, send_sem=k2_send.at[0], recv_sem=k2_recv.at[0],
         device_id=device(D, 1 - H, S), device_id_type=MESH,
     )
     vol_kinds = [(s, f) for s in (0, 1, -1, 2, -2) for f in (1, 0) if (s, f) != (0, 0)]
@@ -265,7 +280,6 @@
             cot_copy(step, far).start()
 
     raw[H, 5:9] = vol[...]
-    cots[0, 1] = cot[...]
     for step in (1, 2, -1, -2):
         low, high = {1: (1, 5), 2: (0, 1), -1: (9, 13), -2: (13, 14)}[step]
 
@@ -282,6 +296,8 @@
     delta[:, 0] = jnp.zeros((4, 128, 128), BF16)
     delta[:, 5] = jnp.zeros((4, 128, 128), BF16)
 
+    loads["k1"].wait()
+    loads["first"].wait()
     base = dot(k1[...], first[...])
     for wp in range(4):
         for dp in range(2):
@@ -293,42 +309,57 @@
 
     def spread_kernel(values, far):
         wide = dot(values, second[0:864, :])
-        bmat[far * 32:far * 32 + 32, :] = wide.astype(BF16)
-        bmat[64 + far * 32:96 + far * 32, :] = pltpu.roll(wide, 32, 1).astype(BF16)
-
+        bmat[far * 64:far * 64 + 32, :] = wide.astype(BF16)
+        bmat[far * 64 + 32:far * 64 + 64, :] = pltpu.roll(wide, 32, 1).astype(BF16)
+
+    loads["k2"].wait()
+    loads["second"].wait()
     spread_kernel(k2[...], 0)
-
-    for step, far in vol_kinds:
-        @pl.when(comes(step))
-        def _():
-            vol_copy(step, far, H if far == 0 else 1 - H).wait_recv()
-
-    def split_row(r, carry):
-        both = jnp.concatenate([raw[0, r], raw[1, r]], axis=0)
-        cut = dot(both, parts[...]).astype(BF16)
+    loads["parts"].wait()
+    loads["order"].wait()
+    loads["cot"].wait()
+    loads["weave"].wait()
+    loads["rows"].wait()
+
+    def split_rows(owner_h, low, high):
+        count = high - low
+        cut = dot(raw[owner_h, low:high].reshape(count * 16, 512), parts[...]).astype(BF16)
         stacked = jnp.concatenate(
             [
                 jnp.concatenate(
-                    [cut[h * 16:h * 16 + 16, s * 128:s * 128 + 128] for h in range(2)], axis=1
+                    [cut[r * 16:r * 16 + 16, s * 128:s * 128 + 128] for s in range(6)], axis=0
                 )
-                for s in range(6)
+                for r in range(count)
             ],
-            axis=0,
+            axis=1,
         )
         placed = dot(order[...], stacked).astype(BF16)
-        for h in range(8):
-            grid[r, 1 + h] = placed[(h % 4) * 32:(h % 4) * 32 + 32, (h // 4) * 128:(h // 4) * 128 + 128]
-        return carry
-
-    lax.fori_loop(0, 14, split_row, 0)
-
-    def first_layer(ld, carry):
+        for r in range(count):
+            for h in range(4):
+                grid[low + r, 1 + owner_h * 4 + h] = placed[
+                    h * 32:h * 32 + 32, r * 128:r * 128 + 128
+                ]
+
+    split_rows(H, 5, 9)
+    for far in (0, 1):
+        for step in (0, 1, -1, 2, -2):
+            if (step, far) != (0, 0):
+                @pl.when(comes(step))
+                def _():
+                    vol_copy(step, far, H if far == 0 else 1 - H).wait_recv()
+        if far == 0:
+            split_rows(H, 0, 5)
+            split_rows(H, 9, 14)
+        else:
+            split_rows(1 - H, 0, 14)
+
+    def first_layer(ld):
         here = 2 * D - 2 + ld
         inside = jnp.logical_and(here >= 0, here < 2 * depth_count)
         for pair in range(2):
             cells = jnp.concatenate(
                 [
-                    grid[pl.ds(2 * ld, 4), 2 * lh:2 * lh + 4].reshape(512, 128)
+                    grid[2 * ld:2 * ld + 4, 2 * lh:2 * lh + 4].reshape(512, 128)
                     for lh in (2 * pair, 2 * pair + 1)
                 ],
                 axis=1,
@@ -351,56 +382,49 @@
                 level[ld, 1 + 2 * pair + i] = jnp.concatenate(
                     [lane_shift(odd, 1), even, odd, lane_shift(even, -1)], axis=0
                 ).astype(BF16)
-        return carry
-
-    lax.fori_loop(0, 6, first_layer, 0)
-
-    k2_copy.wait_recv()
-    spread_kernel(k2_far[...], 1)
-    for step, far in cot_kinds:
-        @pl.when(comes(step))
-        def _():
-            cot_copy(step, far).wait_recv()
-    for kk in range(9):
-        tile = bmat[:, kk * 128:kk * 128 + 128].astype(F32)
-        bmat_t[:, kk * 128:kk * 128 + 128] = tile.T.astype(BF16)
+
+    for ld in (1, 2, 3, 4):
+        first_layer(ld)
+
+    def second_layer(pair, dd, sides):
+        cells = jnp.concatenate(
+            [level[dd:dd + 3, lh:lh + 3].reshape(1152, 128) for lh in (2 * pair, 2 * pair + 1)],
+            axis=1,
+        )
+        low, high = sides[0] * 64, sides[-1] * 64 + 64
+        z = dot(bmat[low:high, :], cells)
+        small = jnp.exp(-jnp.abs(z))
+        more = 1.0 + small
+        turn = 1.0 / more
+        slope = LEAK_SLOPE + (1.0 - LEAK_SLOPE) * jnp.where(z >= 0, turn, small * turn)
+        at = (dd + 1) // 2
+        grads = []
+        for side in sides:
+            grads += [cots[side, at, :, pair * 128:pair * 128 + 128].astype(F32)] * 2
+        grad = jnp.concatenate(grads, axis=0) * 0.125
+        for i in range(2):
+            delta[dd, 1 + 2 * pair + i, low:high] = (
+                grad * slope[:, i * 128:i * 128 + 128]
+            ).astype(BF16)
+        return z, more
 
     for pair in range(2):
         pool_line = jnp.zeros((32, 128), F32)
         pool_more = jnp.ones((32, 128), F32)
-        for dd in range(4):
-            cells = jnp.concatenate(
-                [level[dd:dd + 3, lh:lh + 3].reshape(1152, 128) for lh in (2 * pair, 2 * pair + 1)],
-                axis=1,
-            )
-            z = dot(bmat[...], cells)
-            small = jnp.exp(-jnp.abs(z))
-            more = 1.0 + small
-            turn = 1.0 / more
-            slope = LEAK_SLOPE + (1.0 - LEAK_SLOPE) * jnp.where(z >= 0, turn, small * turn)
-            if dd in (1, 2):
-                line = jnp.maximum(z, LEAK_SLOPE * z)
-                for wp in range(2):
-                    for i in range(2):
-                        box = (slice(wp * 64, wp * 64 + 32), slice(i * 128, i * 128 + 128))
-                        pool_line = pool_line + line[box]
-                        pool_more = pool_more * more[box]
-            at = (dd + 1) // 2
-            near = cots[0, at, :, pair * 128:pair * 128 + 128].astype(F32)
-            away = cots[1, at, :, pair * 128:pair * 128 + 128].astype(F32)
-            grad = jnp.concatenate([near, away, near, away], axis=0) * 0.125
-            for i in range(2):
-                delta[dd, 1 + 2 * pair + i] = (grad * slope[:, i * 128:i * 128 + 128]).astype(BF16)
+        for dd in (1, 2):
+            z, more = second_layer(pair, dd, (0,))
+            line = jnp.maximum(z, LEAK_SLOPE * z)
+            for wp in range(2):
+                for i in range(2):
+                    box = (slice(wp * 32, wp * 32 + 32), slice(i * 128, i * 128 + 128))
+                    pool_line = pool_line + line[box]
+                    pool_more = pool_more * more[box]
         value = 0.125 * (pool_line + (1.0 - LEAK_SLOPE) * jnp.log(pool_more))
         pooled_out[:, pair * 128:pair * 128 + 128] = value.astype(BF16)
 
     spots = [(dd, lh) for dd in (1, 2) for lh in range(4)]
     mine = jnp.concatenate(
-        [
-            jnp.concatenate([delta[dd, 1 + lh, 0:32], delta[dd, 1 + lh, 64:96]], axis=0)
-            for dd, lh in spots
-        ],
-        axis=1,
+        [delta[dd, 1 + lh, 0:64] for dd, lh in spots], axis=1
     )
     folded = []
     for kd in range(3):
@@ -450,6 +474,28 @@
         lax.fori_loop(1, group, body, 0)
 
     each(lambda i: w_copy(i).start())
+
+    first_layer(0)
+    first_layer(5)
+    k2_copy.wait_recv()
+    spread_kernel(k2_far[...], 1)
+    for kk in range(9):
+        tile = bmat[:, kk * 128:kk * 128 + 128].astype(F32)
+        bmat_t[:, kk * 128:kk * 128 + 128] = tile.T.astype(BF16)
+    for step, far in cot_kinds:
+        @pl.when(comes(step))
+        def _():
+            cot_copy(step, far).wait_recv()
+    for pair in range(2):
+        for dd, sides in ((1, (1,)), (2, (1,)), (0, (0, 1)), (3, (0, 1))):
+            second_layer(pair, dd, sides)
+
+    each(lambda i: w_copy(i).wait_recv())
+    chunk = wpart[me]
+    for i in range(1, group):
+        chunk = chunk + wrecv[i]
+    wgath[me] = chunk
+    each(lambda i: g_copy(i).start())
 
     found = []
     for od in range(2):
@@ -476,12 +522,6 @@
     woven = dot(jnp.concatenate(found, axis=0), weave[...]).astype(BF16)
     act_out[...] = dot(rows[...], woven).astype(BF16)
 
-    each(lambda i: w_copy(i).wait_recv())
-    chunk = wpart[me]
-    for i in range(1, group):
-        chunk = chunk + wrecv[i]
-    wgath[me] = chunk
-    each(lambda i: g_copy(i).start())
     each(lambda i: g_arrival(i).wait_recv())
     for r in range(4):
         for q in range(3):
@@ -509,6 +549,7 @@
     scale = 1.0 / float(total_cells) ** 0.5
     vol = jnp.transpose(volume[0], (1, 2, 0, 3)).reshape(4, 16, 512)
     vmem = pl.BlockSpec(memory_space=pltpu.VMEM)
+    hbm = pl.BlockSpec(memory_space=pltpu.HBM)
     dma = pltpu.SemaphoreType.DMA
     pooled_two, weight_grad, act = pl.pallas_call(
         functools.partial(kernel, (depth_count, sample_count), scale),
@@ -517,7 +558,7 @@
             jax.ShapeDtypeStruct((32, 864), F32),
             jax.ShapeDtypeStruct((128, 256), BF16),
         ),
-        in_specs=[vmem] * 10,
+        in_specs=[vmem] + [hbm] * 9,
         out_specs=(vmem,) * 3,
         scratch_shapes=[
             pltpu.VMEM((2, 14, 16, 512), BF16),
@@ -532,11 +573,20 @@
             pltpu.VMEM((group, 8, 256), F32),
             pltpu.VMEM((group, 8, 256), F32),
             pltpu.VMEM((group, 8, 256), F32),
+            pltpu.VMEM((32, 108), BF16),
+            pltpu.VMEM((32, 864), BF16),
+            pltpu.VMEM((512, 768), BF16),
+            pltpu.VMEM((128, 96), BF16),
+            pltpu.VMEM((108, 512), BF16),
+            pltpu.VMEM((1024, 1152), BF16),
+            pltpu.VMEM((256, 256), BF16),
+            pltpu.VMEM((128, 128), BF16),
+            dma((9,)),
             dma((10,)), dma((10,)), dma((6,)), dma((6,)), dma((1,)), dma((1,)),
             dma((group,)), dma((group,)), dma((group,)), dma((group,)),
         ],
         compiler_params=pltpu.CompilerParams(
-            collective_id=0, has_side_effects=True, vmem_limit_bytes=40 * 1024 * 1024
+            collective_id=0, has_side_effects=True, vmem_limit_bytes=62 * 1024 * 1024
         ),
     )(vol, kernel_one, kernel_two, cotangent.reshape(32, 256), *constants())
     return (

time: 48.6 us -> 36.2 us (0.74)
  Pallas kernels: 36.2 us -> 29.3 us
  local copies, waits for them, and re-layouts: 11.2 us -> 5.92 us
    pallas_call x1, Pallas kernels: 36.2 us -> 29.3 us  [one_kernel(): pl.pallas_call(functools.partial(kernel, (depth_count, sample_count), sca...]
    unnamed x20 -> x2, local copies, waits for them, and re-layouts: 9.59 us -> 2.87 us
    reshape x1, local copies, waits for them, and re-layouts: 0.66 us -> 1.5 us  [one_kernel(): act.reshape(1, 32, 2, 2, 256)]
    reshape x1, local copies, waits for them, and re-layouts: 0.02 us -> 0.65 us  [one_kernel(): vol = jnp.transpose(volume[0], (1, 2, 0, 3)).reshape(4, 16, 512)]
where the time goes in v1:
time: 36.2 us; the launch traced here: 35.8 us
  Pallas kernels  29.3 us (81%)
  local copies, waits for them, and re-layouts  5.92 us (16%)
  between operations  0.64 us (2%)
    pallas_call x1, Pallas kernels, one_kernel(): pl.pallas_call(functools.partial(kernel, (depth_count, sample_count), sca...  29.3 us
    unnamed x2, local copies, waits for them, and re-layouts  2.87 us
    reshape x1, local copies, waits for them, and re-layouts, one_kernel(): act.reshape(1, 32, 2, 2, 256)  1.5 us
    transpose x1, local copies, waits for them, and re-layouts, one_kernel(): vol = jnp.transpose(volume[0], (1, 2, 0, 3)).reshape(4, 16, 512)  0.89 us

profile of v1, /device:TPU:0, one launch (start us, length us, event | category | flops | bytes accessed | tf_op | source)
XLA Modules:
  0.0 35.8 jit_solution(8613084226510474427)
XLA Ops:
  0.6 0.9 %copy.13 = bf16[4,4,4,512]{3,2,1,0:T(4,128)(2,1)S(1)} copy(bf16[4,4,4,512]{3,1,0,2:T(4,128)(2,1)} %bitcast.5) | data formatting | bytes 131072 | tf_op jit(solution)/shard_map/transpose | solution.py:550
  1.5 0.7 %reshape.18.vol = bf16[4,16,512]{2,1,0:T(8,128)(2,1)} reshape(bf16[4,4,4,512]{3,2,1,0:T(4,128)(2,1)S(1)} %copy.13) | data formatting | bytes 131072 | tf_op jit(solution)/shard_map/reshape | solution.py:550
  2.2 29.3 %shard_map.121 = (bf16[32,256]{1,0:T(8,128)(2,1)}, f32[32,864]{1,0:T(8,128)}, bf16[128,256]{1,0:T(8,128)(2,1)}) custom-call(bf16[4,16,512]{2,1,0:T(8,128)(2,1)} %reshape.18.vol, bf16[32,108]{1,0:T(8,128)(2,1)} %k1_hbm.1, bf16[32,864]{1,0:T(8,128)(2,1)} %k2_hbm.1, bf16[32,256]{1,0:T(8,128)(2,1)} %bitcast.6, bf16[512,768]{1,0:T(8,128)(2,1)} %constant.12.clone.parts_hbm, ...), custom_call_target="tpu_custom_call" | custom-call | tf_op jit(solution)/shard_map/pallas_call | solution.py:554
  31.4 1.5 %reshape.21 = bf16[1,32,2,2,256]{4,3,2,1,0:T(2,128)(2,1)} reshape(bf16[128,256]{1,0:T(8,128)(2,1)} %get-tuple-element.8) | data formatting | bytes 131072 | tf_op jit(solution)/shard_map/reshape | solution.py:595
  32.9 1.3 %copy.16 = bf16[1,32,1,256]{3,1,2,0:T(8,128)(2,1)} copy(bf16[1,32,1,256]{3,1,2,0:T(8,128)(2,1)} %bitcast.7) | data formatting | bytes 32768
  34.3 1.6 %copy.17 = f32[32,864]{1,0:T(8,128)} copy(f32[32,864]{1,0:T(8,128)} %get-tuple-element.13) | data formatting | bytes 221184
